TPU v7x, 512 devices: a whole 4x4x16 slice. The times are simulated.
512 devices in a mesh: ctx: 32 (over y, x, core), head: 16 (over z).
Axes of the slice: x: 4, y: 4, z: 16, core: 2. Of those that a mesh axis runs over, the one named last changes fastest.
Arguments:
- queries: bfloat16 [8192, 4096], P('ctx', 'head'), may hold values from -50 to 50
- keys: bfloat16 [8192, 4096], P('ctx', 'head'), may hold values from -9 to 9
- values: bfloat16 [8192, 4096], P('ctx', 'head'), may hold values from -9 to 9
- near_blocks: int32 [64, 4], P('ctx'), may hold values from 0 to 63, as said below
- near_count: int32 [64], P('ctx'), may hold values from 1 to 4
- head_scale: float32 [32], P('head'), may hold values from 0.2 to 4.2
- gain: float32 [4096], P('head'), may hold values from 0.5 to 1.5
- cotangent: bfloat16 [8192, 4096], P('ctx', 'head'), may hold values from -6 to 6
Outputs:
- mixed: bfloat16 [8192, 4096], P('ctx', 'head')
- grad_queries: bfloat16 [8192, 4096], P('ctx', 'head')
- grad_keys: bfloat16 [8192, 4096], P('ctx', 'head')
- grad_values: bfloat16 [8192, 4096], P('ctx', 'head')
Inputs may be any that keep to these rules, and one draw needn't show every extreme that they name: near_blocks[b, 0] = b; entries 1 to near_count[b] - 1 are distinct blocks other than b within 2 blocks of b; the later entries equal b.
All inputs are finite; a program needn't handle non-finite values.
Results may differ from a plain program's by a relative error of at most 0.022.
Values may be sent and summed in bfloat16 or wider, within the bound.
A program may use at most 64 MiB of HBM per device.

v0:
```python
import math
import jax
import jax.numpy as jnp
from jax import lax
from jax.sharding import PartitionSpec as P

HEADS = 32
HEAD_SIZE = 128
BLOCK_TOKENS = 128
NEAR_SLOTS = 4
RB = 2
LEV = 5
LOG_TWO = 0.6931471805599453
NEG_BIG = -1e30
NORM_EPS = 1e-05


def padded_2(cells, sides, width):
    for axis, dim in sides:
        count = lax.axis_size(axis)
        ends = count - 1
        head = lax.slice_in_dim(cells, 0, width, axis=dim)
        tail = lax.slice_in_dim(cells, cells.shape[dim] - width, cells.shape[dim], axis=dim)
        cells = jnp.concatenate(
            [
                lax.ppermute(tail, axis, [(i, (i + 1) % count) for i in range(ends)]),
                cells,
                lax.ppermute(head, axis, [((i + 1) % count, i) for i in range(ends)]),
            ],
            axis=dim,
        )
    return cells


def passed_along(value, axis, by):
    size = lax.axis_size(axis)
    pairs = [(i, i + by) for i in range(size) if 0 <= i + by < size]
    return lax.ppermute(value, axis, pairs)


def shortened(value):

    def short(part):
        return part.astype(jnp.bfloat16) if part.dtype == jnp.float32 else part

    return jax.tree.map(short, value)


def from_partner(value, axis, apart):
    mask = 2**apart
    pairs = [(source, source ^ mask) for source in range(lax.axis_size(axis))]
    return lax.ppermute(value, axis, pairs)


def body(queries, keys, values, near_blocks, near_count, head_scale, gain, cotangent):
    tok_rows = queries.shape[0]
    local_cols = queries.shape[1]
    heads_here = local_cols // HEAD_SIZE
    width = HEADS * HEAD_SIZE
    ctx_count = lax.axis_size("ctx")
    device = lax.axis_index("ctx")
    blocks_here = tok_rows // BLOCK_TOKENS
    margin = RB * BLOCK_TOKENS
    extended = blocks_here + 2 * RB
    columns = 2 * local_cols
    softmax_scale = 1.0 / math.sqrt(HEAD_SIZE)
    pair = jnp.concatenate([keys, values], axis=1)
    padded = padded_2(pair, (("ctx", 0),), margin)
    first_block = device * blocks_here - RB
    select = (near_blocks - first_block)[:, :, None] == jnp.arange(extended, dtype=jnp.int32)[
        None, None, :
    ]
    select_flat = select.reshape(blocks_here * NEAR_SLOTS, extended)
    near_pair = jnp.dot(
        select_flat.astype(jnp.bfloat16),
        padded.reshape(extended, BLOCK_TOKENS * columns),
        preferred_element_type=jnp.float32,
    )
    near_pair = near_pair.astype(jnp.bfloat16).reshape(
        blocks_here, NEAR_SLOTS, BLOCK_TOKENS, columns
    )
    valid = jnp.arange(NEAR_SLOTS, dtype=jnp.int32)[None, :] < near_count[:, None]
    key_mask = jnp.repeat(valid, BLOCK_TOKENS, axis=1)[:, None, :]
    factors = [2 ** (level_idx + 1) for level_idx in range(LEV)]
    groups = [min(2 ** (level_idx + 1), ctx_count) for level_idx in range(LEV)]
    pooled = [
        pair.astype(jnp.float32)
        .reshape(tok_rows // factors[level_idx], factors[level_idx], columns)
        .mean(axis=1)
        .astype(jnp.bfloat16)
        for level_idx in range(LEV)
    ]
    steps_count = max(groups).bit_length() - 1
    q_global = device * tok_rows + jnp.arange(tok_rows, dtype=jnp.int32)
    far_masks = []
    for level_idx in range(LEV):
        span_here = groups[level_idx] * tok_rows
        rows_level = span_here // factors[level_idx]
        group_first = device // groups[level_idx] * span_here
        key_first = group_first + jnp.arange(rows_level, dtype=jnp.int32) * factors[level_idx]
        keep = jnp.abs(key_first[None, :] // BLOCK_TOKENS - q_global[:, None] // BLOCK_TOKENS) > RB
        if level_idx > 0:
            prior = groups[level_idx - 1] * tok_rows
            keep = keep & (key_first[None, :] // prior != q_global[:, None] // prior)
        far_masks.append(keep)
    group_pair = list(pooled)
    shared = [level_idx for level_idx in range(LEV) if groups[level_idx] > 1]
    packed = jnp.concatenate([pooled[level_idx] for level_idx in shared], axis=0)
    everyone = lax.all_gather(packed, "ctx", axis=0, tiled=True).reshape(
        ctx_count, packed.shape[0], columns
    )
    offset = 0
    for level_idx in shared:
        count_rows = pooled[level_idx].shape[0]
        piece = everyone[:, offset : offset + count_rows]
        group_start = device // groups[level_idx] * groups[level_idx]
        chosen = lax.dynamic_slice_in_dim(piece, group_start, groups[level_idx], 0)
        group_pair[level_idx] = chosen.reshape(groups[level_idx] * count_rows, columns)
        offset = offset + count_rows
    saved = []
    attn_list = []
    for head_idx in range(heads_here):
        k_cols = slice(head_idx * HEAD_SIZE, (head_idx + 1) * HEAD_SIZE)
        v_cols = slice((heads_here + head_idx) * HEAD_SIZE, (heads_here + head_idx + 1) * HEAD_SIZE)
        q_head = queries[:, k_cols]
        query_blocks = q_head.reshape(blocks_here, BLOCK_TOKENS, HEAD_SIZE)
        near_key_rows = near_pair[:, :, :, k_cols].reshape(
            blocks_here, NEAR_SLOTS * BLOCK_TOKENS, HEAD_SIZE
        )
        near_value_rows = near_pair[:, :, :, v_cols].reshape(
            blocks_here, NEAR_SLOTS * BLOCK_TOKENS, HEAD_SIZE
        )
        near_score_rows = (
            jnp.einsum(
                "mne,mge->mng", query_blocks, near_key_rows, preferred_element_type=jnp.float32
            )
            * softmax_scale
        )
        near_score_rows = jnp.where(key_mask, near_score_rows, NEG_BIG)
        top = jnp.max(near_score_rows, axis=2).reshape(tok_rows)
        coarse_k = [group_pair[level_idx][:, k_cols] for level_idx in range(LEV)]
        coarse_v = [group_pair[level_idx][:, v_cols] for level_idx in range(LEV)]
        s_far = []
        for level_idx in range(LEV):
            scores = (
                jnp.einsum(
                    "td,kd->tk", q_head, coarse_k[level_idx], preferred_element_type=jnp.float32
                )
                * softmax_scale
                + (level_idx + 1) * LOG_TWO
            )
            scores = jnp.where(far_masks[level_idx], scores, NEG_BIG)
            s_far.append(scores)
            top = jnp.maximum(top, jnp.max(scores, axis=1))
        p_near = jnp.where(
            key_mask, jnp.exp(near_score_rows - top.reshape(blocks_here, BLOCK_TOKENS, 1)), 0.0
        )
        total = jnp.sum(p_near, axis=2).reshape(tok_rows)
        p_far = []
        for level_idx in range(LEV):
            exps = jnp.where(far_masks[level_idx], jnp.exp(s_far[level_idx] - top[:, None]), 0.0)
            p_far.append(exps)
            total = total + jnp.sum(exps, axis=1)
        prob_near = p_near / total.reshape(blocks_here, BLOCK_TOKENS, 1)
        near_weight_rows = prob_near.astype(jnp.bfloat16)
        attention_output = jnp.einsum(
            "itp,ipc->itc", near_weight_rows, near_value_rows, preferred_element_type=jnp.float32
        ).reshape(tok_rows, HEAD_SIZE)
        prob_far = []
        weight_far = []
        for level_idx in range(LEV):
            probs = p_far[level_idx] / total[:, None]
            weights_bf = probs.astype(jnp.bfloat16)
            prob_far.append(probs)
            weight_far.append(weights_bf)
            attention_output = attention_output + jnp.dot(
                weights_bf, coarse_v[level_idx], preferred_element_type=jnp.float32
            )
        attn_list.append(attention_output)
        saved.append(
            (
                q_head,
                query_blocks,
                near_key_rows,
                near_value_rows,
                prob_near,
                near_weight_rows,
                coarse_k,
                coarse_v,
                prob_far,
                weight_far,
            )
        )
    scaled = jnp.concatenate(
        [attn_list[head_idx] * head_scale[head_idx] for head_idx in range(heads_here)], axis=1
    )
    squares = lax.psum(jnp.sum(scaled * scaled, axis=1), "head")
    inv = lax.rsqrt(squares / width + NORM_EPS)
    mixed = (scaled * inv[:, None] * gain[None, :]).astype(jnp.bfloat16)
    back = cotangent.astype(jnp.float32) * gain[None, :]
    inner = lax.psum(jnp.sum(back * scaled, axis=1), "head")
    d_scaled = inv[:, None] * (back - scaled * (inv * inv * inner / width)[:, None])
    grad_q_list = []
    near_dk = []
    near_dv = []
    far_dk = [[] for level_idx in range(LEV)]
    far_dv = [[] for level_idx in range(LEV)]
    for head_idx in range(heads_here):
        (
            q_head,
            query_blocks,
            near_key_rows,
            near_value_rows,
            prob_near,
            near_weight_rows,
            coarse_k,
            coarse_v,
            prob_far,
            weight_far,
        ) = saved[head_idx]
        d_out = (
            d_scaled[:, head_idx * HEAD_SIZE : (head_idx + 1) * HEAD_SIZE] * head_scale[head_idx]
        ).astype(jnp.bfloat16)
        delta = jnp.sum(d_out.astype(jnp.float32) * attn_list[head_idx], axis=1)
        block_gradient = d_out.reshape(blocks_here, BLOCK_TOKENS, HEAD_SIZE)
        near_prob_gradient = jnp.einsum(
            "mne,mge->mng", block_gradient, near_value_rows, preferred_element_type=jnp.float32
        )
        near_score_gradient = (
            prob_near * (near_prob_gradient - delta.reshape(blocks_here, BLOCK_TOKENS, 1))
        ).astype(jnp.bfloat16)
        query_gradient = jnp.einsum(
            "itp,ipc->itc", near_score_gradient, near_key_rows, preferred_element_type=jnp.float32
        ).reshape(tok_rows, HEAD_SIZE)
        near_dk.append(
            jnp.einsum(
                "ail,aiz->alz",
                near_score_gradient,
                query_blocks,
                preferred_element_type=jnp.float32,
            )
            * softmax_scale
        )
        near_dv.append(
            jnp.einsum(
                "ail,aiz->alz", near_weight_rows, block_gradient, preferred_element_type=jnp.float32
            )
        )
        for level_idx in range(LEV):
            dp_far = jnp.einsum(
                "td,kd->tk", d_out, coarse_v[level_idx], preferred_element_type=jnp.float32
            )
            ds_far = (prob_far[level_idx] * (dp_far - delta[:, None])).astype(jnp.bfloat16)
            query_gradient = query_gradient + jnp.dot(
                ds_far, coarse_k[level_idx], preferred_element_type=jnp.float32
            )
            far_dk[level_idx].append(
                jnp.einsum("tk,td->kd", ds_far, q_head, preferred_element_type=jnp.float32)
                * softmax_scale
            )
            far_dv[level_idx].append(
                jnp.einsum(
                    "tk,td->kd", weight_far[level_idx], d_out, preferred_element_type=jnp.float32
                )
            )
        grad_q_list.append(query_gradient * softmax_scale)
    contrib = jnp.concatenate(near_dk + near_dv, axis=2).reshape(
        blocks_here * NEAR_SLOTS, BLOCK_TOKENS * columns
    )
    spread_ext = jnp.einsum(
        "xe,xc->ec", select_flat.astype(jnp.float32), contrib, precision=lax.Precision.HIGHEST
    )
    spread_ext = spread_ext.reshape(extended * BLOCK_TOKENS, columns)
    lower_rim = spread_ext[:margin]
    own_rows = spread_ext[margin : margin + tok_rows]
    upper_rim = spread_ext[margin + tok_rows :]
    from_above = passed_along(lower_rim.astype(jnp.bfloat16), "ctx", -1).astype(lower_rim.dtype)
    from_below = passed_along(upper_rim.astype(jnp.bfloat16), "ctx", 1).astype(upper_rim.dtype)
    grad_pair = own_rows + from_above + from_below
    far_grad = [
        jnp.concatenate(far_dk[level_idx] + far_dv[level_idx], axis=1) for level_idx in range(LEV)
    ]
    for bit_idx in reversed(range(steps_count)):
        active = [level_idx for level_idx in range(LEV) if groups[level_idx] > 2**bit_idx]
        upper_half = device // 2**bit_idx % 2 == 1
        sends = []
        keeps = []
        for level_idx in active:
            half_rows = far_grad[level_idx].shape[0] // 2
            lower_part = far_grad[level_idx][:half_rows]
            upper_part = far_grad[level_idx][half_rows:]
            keeps.append(jnp.where(upper_half, upper_part, lower_part))
            sends.append(jnp.where(upper_half, lower_part, upper_part))
        received = from_partner(shortened(jnp.concatenate(sends, axis=0)), "ctx", bit_idx)
        offset = 0
        for position, level_idx in enumerate(active):
            half_rows = keeps[position].shape[0]
            far_grad[level_idx] = keeps[position] + received[offset : offset + half_rows]
            offset = offset + half_rows
    for level_idx in range(LEV):
        factor = factors[level_idx]
        rows_level = far_grad[level_idx].shape[0]
        expanded = jnp.broadcast_to(
            (far_grad[level_idx] / factor)[:, None, :], (rows_level, factor, columns)
        )
        grad_pair = grad_pair + expanded.reshape(tok_rows, columns)
    grad_queries = jnp.concatenate(grad_q_list, axis=1).astype(jnp.bfloat16)
    grad_keys = grad_pair[:, :local_cols].astype(jnp.bfloat16)
    grad_values = grad_pair[:, local_cols:].astype(jnp.bfloat16)
    return (mixed, grad_queries, grad_keys, grad_values)


def solution(mesh):
    return jax.shard_map(
        body,
        mesh=mesh,
        in_specs=(
            P("ctx", "head"),
            P("ctx", "head"),
            P("ctx", "head"),
            P("ctx", None),
            P("ctx"),
            P("head"),
            P("head"),
            P("ctx", "head"),
        ),
        out_specs=(P("ctx", "head"), P("ctx", "head"), P("ctx", "head"), P("ctx", "head")),
        check_vma=False,
    )
```

profile of v0, /device:TPU:1, one launch (start us, length us, event | category | flops | bytes accessed | tf_op | source)
XLA Modules:
  0.0 259.7 jit_solution(10416025845603578630)
XLA Ops:
  13.6 4.5 %collective-permute-start = (bf16[256,512]{1,0:T(8,128)(2,1)S(1)}, bf16[256,512]{1,0:T(8,128)(2,1)S(1)}, u32[]{:S(2)}, u32[]{:S(2)}) collective-permute-start(bf16[256,512]{1,0:T(8,128)(2,1)S(1)} %constant_dynamic-update-slice_fusion), channel_id=1, source_target_pairs={{0,16},{16,32},{32,48},{48,64},{64,80},{80,96},{96,112},{112,128},... | collective-permute-start | bytes 786440 | tf_op jit(solution)/shard_map/ppermute | solution.py:26
  18.1 5.6 %collective-permute-start.1 = (bf16[256,512]{1,0:T(8,128)(2,1)S(1)}, bf16[256,512]{1,0:T(8,128)(2,1)S(1)}, u32[]{:S(2)}, u32[]{:S(2)}) collective-permute-start(bf16[256,512]{1,0:T(8,128)(2,1)S(1)} %constant_dynamic-update-slice_fusion), channel_id=1, source_target_pairs={{16,0},{32,16},{48,32},{64,48},{80,64},{96,80},{112,96},{128,112},... | collective-permute-start | bytes 786440 | tf_op jit(solution)/shard_map/ppermute | solution.py:28
  28.6 1.1 fusion.272
  30.2 56.8 %all-gather.2.cloned.1.call-done = bf16[7936,512]{1,0:T(8,128)(2,1)} async-done(((bf16[248,512]{1,0:T(8,128)(2,1)}), bf16[7936,512]{1,0:T(8,128)(2,1)}) %all-gather.2.cloned.1.call-update) | async-done | bytes 8126480 | tf_op jit(solution)/shard_map/all_gather | solution.py:109
  87.0 2.6 %slice.349 = bf16[32,128,512]{2,1,0:T(8,128)(2,1)S(1)} slice(bf16[32,248,512]{2,1,0:T(8,128)(2,1)} %bitcast.285), slice={[0:32], [0:128], [0:512]} | slice | bytes 8388608 | tf_op jit(solution)/shard_map/slice | solution.py:115
  89.7 1.8 slice.351
  91.5 1.3 slice.353
  92.8 1.1 slice.355
  101.5 1.1 fusion.101
  102.6 1.7 copy.148
  104.3 1.3 convolution_add_fusion.19
  105.6 1.3 convolution_add_fusion.18
  109.0 1.1 fusion.97
  110.1 1.7 copy.267
  111.8 1.2 convolution_add_fusion.14
  113.1 1.3 convolution_add_fusion.13
  115.9 1.5 broadcast_multiply_fusion.1
  117.5 1.6 broadcast_multiply_fusion
  119.8 25.6 %all-reduce = (f32[256]{0:T(256)}, f32[256]{0:T(256)}) all-reduce(f32[256]{0:T(256)} %get-tuple-element.21, f32[256]{0:T(256)} %get-tuple-element.20), channel_id=1, replica_groups=mesh['ctx'=32,'head'=16] {'head'}, use_global_device_ids=true, to_apply=%region_30.31 | all-reduce | flops 512 | bytes 4096 | tf_op jit(solution)/shard_map/psum | solution.py:197
  146.2 1.8 subtract_multiply_fusion
  147.9 2.2 multiply_reduce_fusion.3
  150.2 1.9 fusion.130
  152.1 1.7 fusion.127
  172.3 4.4 %collective-permute-start.4 = (bf16[128,512]{1,0:T(8,128)(2,1)}, bf16[128,512]{1,0:T(8,128)(2,1)}, u32[]{:S(2)}, u32[]{:S(2)}) collective-permute-start(bf16[128,512]{1,0:T(8,128)(2,1)} %select_convert_fusion), channel_id=1, source_target_pairs={{0,256},{16,272},{32,288},{48,304},{64,320},{80,336},{96,352},{112... | collective-permute-start | bytes 393224 | tf_op jit(solution)/shard_map/ppermute | solution.py:52
  180.2 1.7 reshape.810
  181.9 2.8 %fusion.288 = (bf16[6,65536]{1,0:T(8,128)(2,1)S(1)}, f32[6,65536]{1,0:T(8,128)S(1)}) fusion(f32[8,65536]{1,0:T(8,128)} %reshape.810, s32[8]{0:T(128)S(1)} %copy-done.132), kind=kOutput, calls=%fused_computation.486 | convolution fusion | flops 38142000 | bytes 4456480 | tf_op jit(solution)/shard_map/xe,xc->ec/dot_general | solution.py:270
  186.0 9.1 %collective-permute-start.2 = (bf16[256,512]{1,0:T(8,128)(2,1)}, bf16[256,512]{1,0:T(8,128)(2,1)}, u32[]{:S(2)}, u32[]{:S(2)}) collective-permute-start(bf16[256,512]{1,0:T(8,128)(2,1)} %convert_element_type.240), channel_id=1, source_target_pairs={{16,0},{32,16},{48,32},{64,48},{80,64},{96,80},{112,96},{128,112},... | collective-permute-start | bytes 786440 | tf_op jit(solution)/shard_map/ppermute | solution.py:38
  196.0 2.1 collective-permute-start.3
  198.1 1.1 convolution_add_fusion.9
  199.3 1.2 convolution_add_fusion.8
  200.5 1.1 convolution_add_fusion.7
  201.6 1.1 convolution_add_fusion.6
  202.8 1.2 convolution_add_fusion.4
  204.0 1.1 convolution_add_fusion.3
  205.1 1.8 convolution_add_fusion.2
  207.3 1.1 convert_add_fusion.3
  208.5 2.2 collective-permute-start.5
  210.7 4.8 %collective-permute-done.5 = bf16[192,512]{1,0:T(8,128)(2,1)S(1)} collective-permute-done((bf16[192,512]{1,0:T(8,128)(2,1)S(1)}, bf16[192,512]{1,0:T(8,128)(2,1)S(1)}, u32[]{:S(2)}, u32[]{:S(2)}) %collective-permute-start.5) | collective-permute-done | bytes 196640 | tf_op jit(solution)/shard_map/ppermute | solution.py:52
  215.7 5.5 %collective-permute-start.6 = (bf16[224,512]{1,0:T(8,128)(2,1)S(1)}, bf16[224,512]{1,0:T(8,128)(2,1)S(1)}, u32[]{:S(2)}, u32[]{:S(2)}) collective-permute-start(bf16[224,512]{1,0:T(8,128)(2,1)S(1)} %pad_maximum_fusion.9), channel_id=1, source_target_pairs={{0,64},{16,80},{32,96},{48,112},{64,0},{80,16},{96,32},{112,48},{1... | collective-permute-start | bytes 688136 | tf_op jit(solution)/shard_map/ppermute | solution.py:52
  221.9 3.7 %collective-permute-done.6 = bf16[224,512]{1,0:T(8,128)(2,1)S(1)} collective-permute-done((bf16[224,512]{1,0:T(8,128)(2,1)S(1)}, bf16[224,512]{1,0:T(8,128)(2,1)S(1)}, u32[]{:S(2)}, u32[]{:S(2)}) %collective-permute-start.6) | collective-permute-done | bytes 229408 | tf_op jit(solution)/shard_map/ppermute | solution.py:52
  226.5 4.9 %collective-permute-start.7 = (bf16[240,512]{1,0:T(8,128)(2,1)}, bf16[240,512]{1,0:T(8,128)(2,1)}, u32[]{:S(2)}, u32[]{:S(2)}) collective-permute-start(bf16[240,512]{1,0:T(8,128)(2,1)} %pad_maximum_fusion.8), channel_id=1, source_target_pairs={{0,32},{16,48},{32,0},{48,16},{64,96},{80,112},{96,64},{112,80},{1... | collective-permute-start | bytes 737288 | tf_op jit(solution)/shard_map/ppermute | solution.py:52
  231.5 1.7 fusion.61
  234.3 1.5 slice.299
  235.8 1.7 copy.210
  237.5 1.2 convolution_add_fusion.1
  244.7 3.4 %collective-permute-start.8 = (bf16[248,512]{1,0:T(8,128)(2,1)}, bf16[248,512]{1,0:T(8,128)(2,1)S(1)}, u32[]{:S(2)}, u32[]{:S(2)}) collective-permute-start(bf16[248,512]{1,0:T(8,128)(2,1)} %constant_dynamic-update-slice_fusion.4), channel_id=1, source_target_pairs={{0,16},{16,0},{32,48},{48,32},{64,80},{80,64},{96,112},{112,96},{1... | collective-permute-start | bytes 761864 | tf_op jit(solution)/shard_map/ppermute | solution.py:52
  248.1 1.1 fusion.60
  250.9 1.3 fusion.62
  (459 shorter events, 58.3 us)
Async XLA Ops:
  7.2 79.8 %all-gather.2.cloned.1.call-start = ((), (), s32[]{:S(2)}) async-start(), calls=%async_computation | async-start | bytes 8380416 | tf_op jit(solution)/shard_map/all_gather | solution.py:109
  8.3 17.3 %copy-start.130 = (f32[2]{0:T(128)S(1)}, f32[2]{0:T(128)}, u32[]{:S(2)}) copy-start(f32[2]{0:T(128)} %param.13) | copy-start | bytes 28
  8.3 17.9 %copy-start.146 = (s32[2]{0:T(128)S(1)}, s32[2]{0:T(128)}, u32[]{:S(2)}) copy-start(s32[2]{0:T(128)} %param.12) | copy-start | bytes 28
  8.3 18.1 %copy-start.145 = (s32[2,4]{1,0:T(2,128)S(1)}, s32[2,4]{1,0:T(2,128)}, u32[]{:S(2)}) copy-start(s32[2,4]{1,0:T(2,128)} %param.11) | copy-start | bytes 100
  9.2 17.3 %copy-start.71 = (bf16[256,256]{1,0:T(8,128)(2,1)S(1)}, bf16[256,256]{1,0:T(8,128)(2,1)}, u32[]{:S(2)}) copy-start(bf16[256,256]{1,0:T(8,128)(2,1)} %param.15) | copy-start | bytes 393220
  10.3 16.5 %copy-start = (bf16[256,256]{1,0:T(8,128)(2,1)S(1)}, bf16[256,256]{1,0:T(8,128)(2,1)}, u32[]{:S(2)}) copy-start(bf16[256,256]{1,0:T(8,128)(2,1)} %param.8) | copy-start | bytes 393220
  13.6 13.2 %collective-permute-start = (bf16[256,512]{1,0:T(8,128)(2,1)S(1)}, bf16[256,512]{1,0:T(8,128)(2,1)S(1)}, u32[]{:S(2)}, u32[]{:S(2)}) collective-permute-start(bf16[256,512]{1,0:T(8,128)(2,1)S(1)} %constant_dynamic-update-slice_fusion), channel_id=1, source_target_pairs={{0,16},{16,32},{32,48},{48,64},{64,80},{80,96},{96,112},{112,128},... | collective-permute-start | bytes 786440 | tf_op jit(solution)/shard_map/ppermute | solution.py:26
  18.1 8.7 %collective-permute-start.1 = (bf16[256,512]{1,0:T(8,128)(2,1)S(1)}, bf16[256,512]{1,0:T(8,128)(2,1)S(1)}, u32[]{:S(2)}, u32[]{:S(2)}) collective-permute-start(bf16[256,512]{1,0:T(8,128)(2,1)S(1)} %constant_dynamic-update-slice_fusion), channel_id=1, source_target_pairs={{16,0},{32,16},{48,32},{64,48},{80,64},{96,80},{112,96},{128,112},... | collective-permute-start | bytes 786440 | tf_op jit(solution)/shard_map/ppermute | solution.py:28
  23.7 73.8 %copy-start.81 = (s32[256]{0:T(256)}, s32[256]{0:T(256)S(1)}, u32[]{:S(2)}) copy-start(s32[256]{0:T(256)S(1)} %and_select_fusion.12) | copy-start | bytes 3076
  23.8 72.0 %copy-start.86 = (s32[256]{0:T(256)}, s32[256]{0:T(256)S(1)}, u32[]{:S(2)}) copy-start(s32[256]{0:T(256)S(1)} %get-tuple-element.101) | copy-start | bytes 3076
  23.8 72.6 %copy-start.98 = (s32[256]{0:T(256)}, s32[256]{0:T(256)S(1)}, u32[]{:S(2)}) copy-start(s32[256]{0:T(256)S(1)} %get-tuple-element.100) | copy-start | bytes 3076
  23.8 72.5 %copy-start.101 = (s32[256]{0:T(256)}, s32[256]{0:T(256)S(1)}, u32[]{:S(2)}) copy-start(s32[256]{0:T(256)S(1)} %get-tuple-element.98) | copy-start | bytes 3076
  23.8 72.5 %copy-start.104 = (s32[256]{0:T(256)}, s32[256]{0:T(256)S(1)}, u32[]{:S(2)}) copy-start(s32[256]{0:T(256)S(1)} %get-tuple-element.99) | copy-start | bytes 3076
  25.0 70.7 %copy-start.111 = (s32[256]{0:T(256)}, s32[256]{0:T(256)S(1)}, u32[]{:S(2)}) copy-start(s32[256]{0:T(256)S(1)} %get-tuple-element.102) | copy-start | bytes 3076
  25.0 70.7 %copy-start.114 = (s32[256]{0:T(256)}, s32[256]{0:T(256)S(1)}, u32[]{:S(2)}) copy-start(s32[256]{0:T(256)S(1)} %get-tuple-element.103) | copy-start | bytes 3076
  26.4 68.8 %copy-start.133 = (s32[256]{0:T(256)}, s32[256]{0:T(256)S(1)}, u32[]{:S(2)}) copy-start(s32[256]{0:T(256)S(1)} %and_select_fusion.13) | copy-start | bytes 3076
  94.9 63.1 %copy-start.10 = (bf16[256,512]{1,0:T(8,128)(2,1)}, bf16[256,512]{1,0:T(8,128)(2,1)S(1)}, u32[]{:S(2)}) copy-start(bf16[256,512]{1,0:T(8,128)(2,1)S(1)} %slice_bitcast_fusion) | copy-start | bytes 786436
  94.9 68.7 %copy-start.7 = (bf16[2,128,512]{2,1,0:T(8,128)(2,1)}, bf16[2,128,512]{2,1,0:T(8,128)(2,1)S(1)}, u32[]{:S(2)}) copy-start(bf16[2,128,512]{2,1,0:T(8,128)(2,1)S(1)} %constant_dynamic-slice_fusion.3) | copy-start | bytes 786436
  95.2 16.6 %copy-start.40 = (f32[256,256]{0,1:T(8,128)}, f32[256,256]{0,1:T(8,128)S(1)}, u32[]{:S(2)}) copy-start(f32[256,256]{0,1:T(8,128)S(1)} %get-tuple-element.83) | copy-start | bytes 786436
  95.4 65.3 %copy-start.8 = (bf16[4,64,512]{2,1,0:T(8,128)(2,1)}, bf16[4,64,512]{2,1,0:T(8,128)(2,1)S(1)}, u32[]{:S(2)}) copy-start(bf16[4,64,512]{2,1,0:T(8,128)(2,1)S(1)} %constant_dynamic-slice_fusion.2) | copy-start | bytes 786436
  96.1 60.1 %copy-start.9 = (bf16[8,32,512]{2,1,0:T(8,128)(2,1)}, bf16[8,32,512]{2,1,0:T(8,128)(2,1)S(1)}, u32[]{:S(2)}) copy-start(bf16[8,32,512]{2,1,0:T(8,128)(2,1)S(1)} %constant_dynamic-slice_fusion.1) | copy-start | bytes 786436
  96.7 104.9 %copy-start.6 = (bf16[16,16,512]{2,1,0:T(8,128)(2,1)}, bf16[16,16,512]{2,1,0:T(8,128)(2,1)S(1)}, u32[]{:S(2)}) copy-start(bf16[16,16,512]{2,1,0:T(8,128)(2,1)S(1)} %constant_dynamic-slice_fusion) | copy-start | bytes 786436
  117.5 28.7 %copy-start.28 = (f32[256,128]{0,1:T(8,128)}, f32[256,128]{0,1:T(8,128)S(1)}, u32[]{:S(2)}) copy-start(f32[256,128]{0,1:T(8,128)S(1)} %get-tuple-element.88) | copy-start | bytes 393220
  119.1 27.1 %copy-start.29 = (f32[256,128]{0,1:T(8,128)}, f32[256,128]{0,1:T(8,128)S(1)}, u32[]{:S(2)}) copy-start(f32[256,128]{0,1:T(8,128)S(1)} %get-tuple-element.86) | copy-start | bytes 393220
  155.9 11.9 %copy-start.22 = (bf16[256,256]{0,1:T(8,128)(2,1)}, bf16[256,256]{0,1:T(8,128)(2,1)S(1)}, u32[]{:S(2)}) copy-start(bf16[256,256]{0,1:T(8,128)(2,1)S(1)} %fusion.50) | copy-start | bytes 393220
  156.2 13.3 %copy-start.21 = (bf16[256,256]{0,1:T(8,128)(2,1)}, bf16[256,256]{0,1:T(8,128)(2,1)S(1)}, u32[]{:S(2)}) copy-start(bf16[256,256]{0,1:T(8,128)(2,1)S(1)} %fusion.51) | copy-start | bytes 393220
  156.4 12.2 %copy-start.19 = (bf16[256,256]{0,1:T(8,128)(2,1)}, bf16[256,256]{0,1:T(8,128)(2,1)S(1)}, u32[]{:S(2)}) copy-start(bf16[256,256]{0,1:T(8,128)(2,1)S(1)} %fusion.55) | copy-start | bytes 393220
  157.2 13.2 %copy-start.16 = (bf16[256,256]{0,1:T(8,128)(2,1)}, bf16[256,256]{0,1:T(8,128)(2,1)S(1)}, u32[]{:S(2)}) copy-start(bf16[256,256]{0,1:T(8,128)(2,1)S(1)} %fusion.56) | copy-start | bytes 393220
  158.0 13.2 %copy-start.17 = (bf16[256,256]{0,1:T(8,128)(2,1)}, bf16[256,256]{0,1:T(8,128)(2,1)S(1)}, u32[]{:S(2)}) copy-start(bf16[256,256]{0,1:T(8,128)(2,1)S(1)} %fusion.52) | copy-start | bytes 393220
  158.7 12.6 %copy-start.14 = (bf16[256,256]{0,1:T(8,128)(2,1)}, bf16[256,256]{0,1:T(8,128)(2,1)S(1)}, u32[]{:S(2)}) copy-start(bf16[256,256]{0,1:T(8,128)(2,1)S(1)} %fusion.57) | copy-start | bytes 393220
  160.8 15.9 %copy-start.25 = (bf16[256,256]{0,1:T(8,128)(2,1)}, bf16[256,256]{0,1:T(8,128)(2,1)S(1)}, u32[]{:S(2)}) copy-start(bf16[256,256]{0,1:T(8,128)(2,1)S(1)} %fusion.49) | copy-start | bytes 393220
  161.5 16.0 %copy-start.23 = (bf16[256,256]{0,1:T(8,128)(2,1)}, bf16[256,256]{0,1:T(8,128)(2,1)S(1)}, u32[]{:S(2)}) copy-start(bf16[256,256]{0,1:T(8,128)(2,1)S(1)} %fusion.54) | copy-start | bytes 393220
  163.6 14.8 %copy-start.27 = (bf16[256,256]{0,1:T(8,128)(2,1)}, bf16[256,256]{0,1:T(8,128)(2,1)S(1)}, u32[]{:S(2)}) copy-start(bf16[256,256]{0,1:T(8,128)(2,1)S(1)} %fusion.48) | copy-start | bytes 393220
  163.8 15.4 %copy-start.26 = (bf16[256,256]{0,1:T(8,128)(2,1)}, bf16[256,256]{0,1:T(8,128)(2,1)S(1)}, u32[]{:S(2)}) copy-start(bf16[256,256]{0,1:T(8,128)(2,1)S(1)} %fusion.53) | copy-start | bytes 393220
  172.3 35.1 %collective-permute-start.4 = (bf16[128,512]{1,0:T(8,128)(2,1)}, bf16[128,512]{1,0:T(8,128)(2,1)}, u32[]{:S(2)}, u32[]{:S(2)}) collective-permute-start(bf16[128,512]{1,0:T(8,128)(2,1)} %select_convert_fusion), channel_id=1, source_target_pairs={{0,256},{16,272},{32,288},{48,304},{64,320},{80,336},{96,352},{112... | collective-permute-start | bytes 393224 | tf_op jit(solution)/shard_map/ppermute | solution.py:52
  184.6 13.4 %copy-start.12 = (f32[2,128,128]{2,1,0:T(8,128)S(1)}, f32[2,128,128]{2,1,0:T(8,128)}, u32[]{:S(2)}) copy-start(f32[2,128,128]{2,1,0:T(8,128)} %fusion.289) | copy-start | bytes 393220
  186.0 16.8 %copy-start.13 = (f32[2,128,128]{2,1,0:T(8,128)S(1)}, f32[2,128,128]{2,1,0:T(8,128)}, u32[]{:S(2)}) copy-start(f32[2,128,128]{2,1,0:T(8,128)} %fusion.290) | copy-start | bytes 393220
  186.0 64.9 %collective-permute-start.2 = (bf16[256,512]{1,0:T(8,128)(2,1)}, bf16[256,512]{1,0:T(8,128)(2,1)}, u32[]{:S(2)}, u32[]{:S(2)}) collective-permute-start(bf16[256,512]{1,0:T(8,128)(2,1)} %convert_element_type.240), channel_id=1, source_target_pairs={{16,0},{32,16},{48,32},{64,48},{80,64},{96,80},{112,96},{128,112},... | collective-permute-start | bytes 786440 | tf_op jit(solution)/shard_map/ppermute | solution.py:38
  196.0 54.8 %collective-permute-start.3 = (bf16[256,512]{1,0:T(8,128)(2,1)}, bf16[256,512]{1,0:T(8,128)(2,1)}, u32[]{:S(2)}, u32[]{:S(2)}) collective-permute-start(bf16[256,512]{1,0:T(8,128)(2,1)} %convert_element_type.242), channel_id=1, source_target_pairs={{0,16},{16,32},{32,48},{48,64},{64,80},{80,96},{96,112},{112,128},... | collective-permute-start | bytes 786440 | tf_op jit(solution)/shard_map/ppermute | solution.py:38
  208.5 7.1 %collective-permute-start.5 = (bf16[192,512]{1,0:T(8,128)(2,1)S(1)}, bf16[192,512]{1,0:T(8,128)(2,1)S(1)}, u32[]{:S(2)}, u32[]{:S(2)}) collective-permute-start(bf16[192,512]{1,0:T(8,128)(2,1)S(1)} %pad_maximum_fusion.10), channel_id=1, source_target_pairs={{0,128},{16,144},{32,160},{48,176},{64,192},{80,208},{96,224},{112... | collective-permute-start | bytes 589832 | tf_op jit(solution)/shard_map/ppermute | solution.py:52
  215.6 15.9 %copy-start.18 = (bf16[256,256]{0,1:T(8,128)(2,1)S(1)}, bf16[256,256]{0,1:T(8,128)(2,1)}, u32[]{:S(2)}) copy-start(bf16[256,256]{0,1:T(8,128)(2,1)} %copy-done.17) | copy-start | bytes 393220
  215.7 9.9 %collective-permute-start.6 = (bf16[224,512]{1,0:T(8,128)(2,1)S(1)}, bf16[224,512]{1,0:T(8,128)(2,1)S(1)}, u32[]{:S(2)}, u32[]{:S(2)}) collective-permute-start(bf16[224,512]{1,0:T(8,128)(2,1)S(1)} %pad_maximum_fusion.9), channel_id=1, source_target_pairs={{0,64},{16,80},{32,96},{48,112},{64,0},{80,16},{96,32},{112,48},{1... | collective-permute-start | bytes 688136 | tf_op jit(solution)/shard_map/ppermute | solution.py:52
  225.7 14.0 %copy-start.5 = (f32[64,512]{1,0:T(8,128)}, f32[64,512]{1,0:T(8,128)S(1)}, u32[]{:S(2)}) copy-start(f32[64,512]{1,0:T(8,128)S(1)} %convert_add_fusion.5) | copy-start | bytes 393220
  225.7 13.0 %copy-start.4 = (f32[256,512]{1,0:T(8,128)S(1)}, f32[256,512]{1,0:T(8,128)}, u32[]{:S(2)}) copy-start(f32[256,512]{1,0:T(8,128)} %copy-done.3) | copy-start | bytes 1572868
  226.5 12.2 %collective-permute-start.7 = (bf16[240,512]{1,0:T(8,128)(2,1)}, bf16[240,512]{1,0:T(8,128)(2,1)}, u32[]{:S(2)}, u32[]{:S(2)}) collective-permute-start(bf16[240,512]{1,0:T(8,128)(2,1)} %pad_maximum_fusion.8), channel_id=1, source_target_pairs={{0,32},{16,48},{32,0},{48,16},{64,96},{80,112},{96,64},{112,80},{1... | collective-permute-start | bytes 737288 | tf_op jit(solution)/shard_map/ppermute | solution.py:52
  234.3 13.8 %copy-start.15 = (bf16[256,256]{0,1:T(8,128)(2,1)S(1)}, bf16[256,256]{0,1:T(8,128)(2,1)}, u32[]{:S(2)}) copy-start(bf16[256,256]{0,1:T(8,128)(2,1)} %copy-done.14) | copy-start | bytes 393220
  234.3 14.9 %copy-start.66 = (bf16[256,128]{1,0:T(8,128)(2,1)S(1)}, bf16[256,128]{1,0:T(8,128)(2,1)}, u32[]{:S(2)}) copy-start(bf16[256,128]{1,0:T(8,128)(2,1)} %fusion.61) | copy-start | bytes 196612
  244.7 5.2 %collective-permute-start.8 = (bf16[248,512]{1,0:T(8,128)(2,1)}, bf16[248,512]{1,0:T(8,128)(2,1)S(1)}, u32[]{:S(2)}, u32[]{:S(2)}) collective-permute-start(bf16[248,512]{1,0:T(8,128)(2,1)} %constant_dynamic-update-slice_fusion.4), channel_id=1, source_target_pairs={{0,16},{16,0},{32,48},{48,32},{64,80},{80,64},{96,112},{112,96},{1... | collective-permute-start | bytes 761864 | tf_op jit(solution)/shard_map/ppermute | solution.py:52
  (110 other events, 407.6 us)
Sparse Core Ops, SparseCore 0:
  13.6 73.3 all-gather.1
where the time goes:
time: 261 us; the launch traced here: 260 us
  waiting for transfers between devices  65.4 us (25%)
  matrix products  55.1 us (21%)
  starting transfers between devices  41.8 us (16%)
  local copies, waits for them, and re-layouts  30.9 us (12%)
  blocking collectives  25.6 us (10%)
  other arithmetic  24.1 us (9%)
  between operations  16.8 us (6%)
    all_gather x1, waiting for transfers between devices, body(): lax.all_gather(packed, 'ctx', axis=0, tiled=True)  56.8 us
    psum x1, blocking collectives, body(): squares = lax.psum(jnp.sum(scaled * scaled, axis=1), 'head')  25.6 us
    ppermute x5, starting transfers between devices, from_partner(): return lax.ppermute(value, axis, pairs)  20.5 us
    dot_general x10, matrix products, body(): jnp.dot(ds_far, coarse_k[level_idx], preferred_element_type=jnp.float32)  12.6 us
    dot_general x10, matrix products, body(): jnp.dot(weights_bf, coarse_v[level_idx], preferred_element_type=jnp.float32)  11.6 us
    ppermute x2, starting transfers between devices, passed_along(): return lax.ppermute(value, axis, pairs)  11.2 us
    dot_general x10, matrix products, body(): jnp.einsum('tk,td->kd', weight_far[level_idx], d_out, preferred_element_t...  9.72 us
    ppermute x5, waiting for transfers between devices, from_partner(): return lax.ppermute(value, axis, pairs)  8.53 us
  transfers between devices with their start and end apart: 10, of which 3 were waited for; matrix products, arithmetic and copies ran while one was open for 17% of the time, Pallas kernels for 0%

commit v1 on v0

--- a/solution.py
+++ b/solution.py
@@ -194,7 +194,7 @@
     scaled = jnp.concatenate(
         [attn_list[head_idx] * head_scale[head_idx] for head_idx in range(heads_here)], axis=1
     )
-    squares = lax.psum(jnp.sum(scaled * scaled, axis=1), "head")
+    squares = jnp.sum(lax.all_gather(jnp.sum(scaled * scaled, axis=1), "head"), axis=0)
     inv = lax.rsqrt(squares / width + NORM_EPS)
     mixed = (scaled * inv[:, None] * gain[None, :]).astype(jnp.bfloat16)
     back = cotangent.astype(jnp.float32) * gain[None, :]

time: 261 us -> 289 us (1.11)
  blocking collectives: 25.6 us -> 45.3 us
  starting transfers between devices: 41.8 us -> 49.4 us
    all_gather x0 -> x1, blocking collectives: none -> 23.7 us  [body(): lax.all_gather(jnp.sum(scaled * scaled, axis=1), 'head')]
    ppermute x2, starting transfers between devices: 11.2 us -> 18.8 us  [passed_along(): return lax.ppermute(value, axis, pairs)]
    psum x1, blocking collectives: 25.6 us -> 21.6 us  [body(): inner = lax.psum(jnp.sum(back * scaled, axis=1), 'head')]
  transfers between devices with their start and end apart: 10 -> 10, of which waited for: 3 -> 3; matrix products, arithmetic and copies ran while one was open for 17% -> 15% of each run, Pallas kernels for 0% -> 0%
where the time goes in v1:
time: 289 us; the launch traced here: 287 us
  waiting for transfers between devices  65.4 us (23%)
  matrix products  54.5 us (19%)
  starting transfers between devices  49.4 us (17%)
  blocking collectives  45.3 us (16%)
  local copies, waits for them, and re-layouts  30.9 us (11%)
  other arithmetic  24.6 us (9%)
  between operations  16.9 us (6%)
    all_gather x1, waiting for transfers between devices, body(): lax.all_gather(packed, 'ctx', axis=0, tiled=True)  56.9 us
    all_gather x1, blocking collectives, body(): lax.all_gather(jnp.sum(scaled * scaled, axis=1), 'head')  23.7 us
    psum x1, blocking collectives, body(): inner = lax.psum(jnp.sum(back * scaled, axis=1), 'head')  21.6 us
    ppermute x5, starting transfers between devices, from_partner(): return lax.ppermute(value, axis, pairs)  20.5 us
    ppermute x2, starting transfers between devices, passed_along(): return lax.ppermute(value, axis, pairs)  18.8 us
    dot_general x10, matrix products, body(): jnp.dot(ds_far, coarse_k[level_idx], preferred_element_type=jnp.float32)  12.6 us
    dot_general x10, matrix products, body(): jnp.dot(weights_bf, coarse_v[level_idx], preferred_element_type=jnp.float32)  11.7 us
    dot_general x10, matrix products, body(): jnp.einsum('tk,td->kd', weight_far[level_idx], d_out, preferred_element_t...  9.01 us
  transfers between devices with their start and end apart: 10, of which 3 were waited for; matrix products, arithmetic and copies ran while one was open for 15% of the time, Pallas kernels for 0%

profile of v1, /device:TPU:1, one launch (start us, length us, event | category | flops | bytes accessed | tf_op | source)
XLA Modules:
  0.0 287.0 jit_solution(17350458579066987253)
XLA Ops:
  13.6 4.5 %collective-permute-start = (bf16[256,512]{1,0:T(8,128)(2,1)S(1)}, bf16[256,512]{1,0:T(8,128)(2,1)S(1)}, u32[]{:S(2)}, u32[]{:S(2)}) collective-permute-start(bf16[256,512]{1,0:T(8,128)(2,1)S(1)} %constant_dynamic-update-slice_fusion), channel_id=1, source_target_pairs={{0,16},{16,32},{32,48},{48,64},{64,80},{80,96},{96,112},{112,128},... | collective-permute-start | bytes 786440 | tf_op jit(solution)/shard_map/ppermute | solution.py:26
  18.1 5.6 %collective-permute-start.1 = (bf16[256,512]{1,0:T(8,128)(2,1)S(1)}, bf16[256,512]{1,0:T(8,128)(2,1)S(1)}, u32[]{:S(2)}, u32[]{:S(2)}) collective-permute-start(bf16[256,512]{1,0:T(8,128)(2,1)S(1)} %constant_dynamic-update-slice_fusion), channel_id=1, source_target_pairs={{16,0},{32,16},{48,32},{64,48},{80,64},{96,80},{112,96},{128,112},... | collective-permute-start | bytes 786440 | tf_op jit(solution)/shard_map/ppermute | solution.py:28
  28.5 1.1 fusion.272
  30.1 56.9 %all-gather.4.cloned.1.call-done = bf16[7936,512]{1,0:T(8,128)(2,1)} async-done(((bf16[248,512]{1,0:T(8,128)(2,1)}), bf16[7936,512]{1,0:T(8,128)(2,1)}) %all-gather.4.cloned.1.call-update) | async-done | bytes 8126480 | tf_op jit(solution)/shard_map/all_gather | solution.py:109
  87.0 2.6 slice.349
  89.7 1.8 slice.351
  91.5 1.3 slice.353
  92.8 1.1 slice.355
  101.5 1.1 fusion.101
  102.6 1.7 copy.148
  104.3 1.3 convolution_add_fusion.19
  105.6 1.3 convolution_add_fusion.18
  109.0 1.1 fusion.97
  110.1 1.7 copy.267
  111.8 1.2 convolution_add_fusion.14
  113.1 1.3 convolution_add_fusion.13
  115.9 1.6 broadcast_multiply_fusion.1
  117.5 1.6 broadcast_multiply_fusion
  119.8 23.7 %all-gather.1 = f32[16,1,256]{2,1,0:T(1,128)S(1)} all-gather(f32[1,1,256]{2,1,0:T(1,128)S(1)} %bitcast.356), channel_id=2, replica_groups=mesh['ctx'=32,'head'=16] {'head'}, dimensions={0}, use_global_device_ids=true | all-gather | bytes 17408 | tf_op jit(solution)/shard_map/all_gather | solution.py:197
  143.5 21.6 %psum.7 = f32[256]{0:T(256)} all-reduce(f32[256]{0:T(256)} %get-tuple-element.20), channel_id=1, replica_groups=mesh['ctx'=32,'head'=16] {'head'}, use_global_device_ids=true, to_apply=%region_32.33 | all-reduce | flops 256 | bytes 2048 | tf_op jit(solution)/shard_map/psum | solution.py:201
  166.4 1.8 subtract_multiply_fusion
  168.2 2.3 multiply_reduce_fusion.3
  170.5 2.0 fusion.130
  191.9 4.4 %collective-permute-start.4 = (bf16[128,512]{1,0:T(8,128)(2,1)}, bf16[128,512]{1,0:T(8,128)(2,1)}, u32[]{:S(2)}, u32[]{:S(2)}) collective-permute-start(bf16[128,512]{1,0:T(8,128)(2,1)} %select_convert_fusion), channel_id=1, source_target_pairs={{0,256},{16,272},{32,288},{48,304},{64,320},{80,336},{96,352},{112... | collective-permute-start | bytes 393224 | tf_op jit(solution)/shard_map/ppermute | solution.py:52
  199.9 1.7 reshape.814
  201.5 2.8 fusion.288
  205.6 16.7 %collective-permute-start.2 = (bf16[256,512]{1,0:T(8,128)(2,1)}, bf16[256,512]{1,0:T(8,128)(2,1)}, u32[]{:S(2)}, u32[]{:S(2)}) collective-permute-start(bf16[256,512]{1,0:T(8,128)(2,1)} %convert_element_type.240), channel_id=1, source_target_pairs={{16,0},{32,16},{48,32},{64,48},{80,64},{96,80},{112,96},{128,112},... | collective-permute-start | bytes 786440 | tf_op jit(solution)/shard_map/ppermute | solution.py:38
  223.3 2.1 collective-permute-start.3
  225.3 1.1 convolution_add_fusion.9
  226.5 1.2 convolution_add_fusion.8
  227.7 1.1 convolution_add_fusion.7
  228.9 1.1 convolution_add_fusion.6
  230.0 1.2 convolution_add_fusion.4
  232.4 1.8 convolution_add_fusion.2
  234.6 1.1 convert_add_fusion.3
  235.7 2.2 collective-permute-start.5
  238.0 4.8 %collective-permute-done.5 = bf16[192,512]{1,0:T(8,128)(2,1)S(1)} collective-permute-done((bf16[192,512]{1,0:T(8,128)(2,1)S(1)}, bf16[192,512]{1,0:T(8,128)(2,1)S(1)}, u32[]{:S(2)}, u32[]{:S(2)}) %collective-permute-start.5) | collective-permute-done | bytes 196640 | tf_op jit(solution)/shard_map/ppermute | solution.py:52
  243.0 5.5 %collective-permute-start.6 = (bf16[224,512]{1,0:T(8,128)(2,1)S(1)}, bf16[224,512]{1,0:T(8,128)(2,1)S(1)}, u32[]{:S(2)}, u32[]{:S(2)}) collective-permute-start(bf16[224,512]{1,0:T(8,128)(2,1)S(1)} %pad_maximum_fusion.9), channel_id=1, source_target_pairs={{0,64},{16,80},{32,96},{48,112},{64,0},{80,16},{96,32},{112,48},{1... | collective-permute-start | bytes 688136 | tf_op jit(solution)/shard_map/ppermute | solution.py:52
  249.2 3.7 %collective-permute-done.6 = bf16[224,512]{1,0:T(8,128)(2,1)S(1)} collective-permute-done((bf16[224,512]{1,0:T(8,128)(2,1)S(1)}, bf16[224,512]{1,0:T(8,128)(2,1)S(1)}, u32[]{:S(2)}, u32[]{:S(2)}) %collective-permute-start.6) | collective-permute-done | bytes 229408 | tf_op jit(solution)/shard_map/ppermute | solution.py:52
  253.8 4.9 %collective-permute-start.7 = (bf16[240,512]{1,0:T(8,128)(2,1)}, bf16[240,512]{1,0:T(8,128)(2,1)}, u32[]{:S(2)}, u32[]{:S(2)}) collective-permute-start(bf16[240,512]{1,0:T(8,128)(2,1)} %pad_maximum_fusion.8), channel_id=1, source_target_pairs={{0,32},{16,48},{32,0},{48,16},{64,96},{80,112},{96,64},{112,80},{1... | collective-permute-start | bytes 737288 | tf_op jit(solution)/shard_map/ppermute | solution.py:52
  258.8 1.7 fusion.61
  260.5 1.1 slice.379
  261.5 1.5 slice.299
  263.1 1.7 copy.210
  264.7 1.2 convolution_add_fusion.1
  271.9 3.4 %collective-permute-start.8 = (bf16[248,512]{1,0:T(8,128)(2,1)}, bf16[248,512]{1,0:T(8,128)(2,1)S(1)}, u32[]{:S(2)}, u32[]{:S(2)}) collective-permute-start(bf16[248,512]{1,0:T(8,128)(2,1)} %constant_dynamic-update-slice_fusion.4), channel_id=1, source_target_pairs={{0,16},{16,0},{32,48},{48,32},{64,80},{80,64},{96,112},{112,96},{1... | collective-permute-start | bytes 761864 | tf_op jit(solution)/shard_map/ppermute | solution.py:52
  275.4 1.1 fusion.60
  278.1 1.3 fusion.62
  (473 shorter events, 59.6 us)
Async XLA Ops:
  7.2 79.8 %all-gather.4.cloned.1.call-start = ((), (), s32[]{:S(2)}) async-start(), calls=%async_computation | async-start | bytes 8380416 | tf_op jit(solution)/shard_map/all_gather | solution.py:109
  8.3 17.3 %copy-start.136 = (f32[2]{0:T(128)S(1)}, f32[2]{0:T(128)}, u32[]{:S(2)}) copy-start(f32[2]{0:T(128)} %param.13) | copy-start | bytes 28
  8.3 17.9 %copy-start.152 = (s32[2]{0:T(128)S(1)}, s32[2]{0:T(128)}, u32[]{:S(2)}) copy-start(s32[2]{0:T(128)} %param.12) | copy-start | bytes 28
  8.3 18.0 %copy-start.151 = (s32[2,4]{1,0:T(2,128)S(1)}, s32[2,4]{1,0:T(2,128)}, u32[]{:S(2)}) copy-start(s32[2,4]{1,0:T(2,128)} %param.11) | copy-start | bytes 100
  9.2 17.2 %copy-start.71 = (bf16[256,256]{1,0:T(8,128)(2,1)S(1)}, bf16[256,256]{1,0:T(8,128)(2,1)}, u32[]{:S(2)}) copy-start(bf16[256,256]{1,0:T(8,128)(2,1)} %param.15) | copy-start | bytes 393220
  10.3 16.4 %copy-start = (bf16[256,256]{1,0:T(8,128)(2,1)S(1)}, bf16[256,256]{1,0:T(8,128)(2,1)}, u32[]{:S(2)}) copy-start(bf16[256,256]{1,0:T(8,128)(2,1)} %param.8) | copy-start | bytes 393220
  13.6 13.2 %collective-permute-start = (bf16[256,512]{1,0:T(8,128)(2,1)S(1)}, bf16[256,512]{1,0:T(8,128)(2,1)S(1)}, u32[]{:S(2)}, u32[]{:S(2)}) collective-permute-start(bf16[256,512]{1,0:T(8,128)(2,1)S(1)} %constant_dynamic-update-slice_fusion), channel_id=1, source_target_pairs={{0,16},{16,32},{32,48},{48,64},{64,80},{80,96},{96,112},{112,128},... | collective-permute-start | bytes 786440 | tf_op jit(solution)/shard_map/ppermute | solution.py:26
  18.1 8.6 %collective-permute-start.1 = (bf16[256,512]{1,0:T(8,128)(2,1)S(1)}, bf16[256,512]{1,0:T(8,128)(2,1)S(1)}, u32[]{:S(2)}, u32[]{:S(2)}) collective-permute-start(bf16[256,512]{1,0:T(8,128)(2,1)S(1)} %constant_dynamic-update-slice_fusion), channel_id=1, source_target_pairs={{16,0},{32,16},{48,32},{64,48},{80,64},{96,80},{112,96},{128,112},... | collective-permute-start | bytes 786440 | tf_op jit(solution)/shard_map/ppermute | solution.py:28
  23.7 73.8 %copy-start.87 = (s32[256]{0:T(256)}, s32[256]{0:T(256)S(1)}, u32[]{:S(2)}) copy-start(s32[256]{0:T(256)S(1)} %and_select_fusion.12) | copy-start | bytes 3076
  23.8 72.0 %copy-start.91 = (s32[256]{0:T(256)}, s32[256]{0:T(256)S(1)}, u32[]{:S(2)}) copy-start(s32[256]{0:T(256)S(1)} %get-tuple-element.99) | copy-start | bytes 3076
  23.8 72.6 %copy-start.103 = (s32[256]{0:T(256)}, s32[256]{0:T(256)S(1)}, u32[]{:S(2)}) copy-start(s32[256]{0:T(256)S(1)} %get-tuple-element.98) | copy-start | bytes 3076
  23.8 72.5 %copy-start.107 = (s32[256]{0:T(256)}, s32[256]{0:T(256)S(1)}, u32[]{:S(2)}) copy-start(s32[256]{0:T(256)S(1)} %get-tuple-element.96) | copy-start | bytes 3076
  23.8 72.5 %copy-start.110 = (s32[256]{0:T(256)}, s32[256]{0:T(256)S(1)}, u32[]{:S(2)}) copy-start(s32[256]{0:T(256)S(1)} %get-tuple-element.97) | copy-start | bytes 3076
  24.9 70.8 %copy-start.117 = (s32[256]{0:T(256)}, s32[256]{0:T(256)S(1)}, u32[]{:S(2)}) copy-start(s32[256]{0:T(256)S(1)} %get-tuple-element.100) | copy-start | bytes 3076
  24.9 70.8 %copy-start.120 = (s32[256]{0:T(256)}, s32[256]{0:T(256)S(1)}, u32[]{:S(2)}) copy-start(s32[256]{0:T(256)S(1)} %get-tuple-element.101) | copy-start | bytes 3076
  26.3 68.8 %copy-start.139 = (s32[256]{0:T(256)}, s32[256]{0:T(256)S(1)}, u32[]{:S(2)}) copy-start(s32[256]{0:T(256)S(1)} %and_select_fusion.13) | copy-start | bytes 3076
  26.5 82.5 %copy-start.80 = (pred[1,2,4,128]{3,1,2,0:T(4,128)(4,1)}, pred[1,2,4,128]{3,1,2,0:T(4,128)(4,1)S(1)}, u32[]{:S(2)}) copy-start(pred[1,2,4,128]{3,1,2,0:T(4,128)(4,1)S(1)} %copy.289) | copy-start | bytes 3076
  94.9 82.8 %copy-start.10 = (bf16[256,512]{1,0:T(8,128)(2,1)}, bf16[256,512]{1,0:T(8,128)(2,1)S(1)}, u32[]{:S(2)}) copy-start(bf16[256,512]{1,0:T(8,128)(2,1)S(1)} %slice_bitcast_fusion) | copy-start | bytes 786436
  94.9 88.3 %copy-start.7 = (bf16[2,128,512]{2,1,0:T(8,128)(2,1)}, bf16[2,128,512]{2,1,0:T(8,128)(2,1)S(1)}, u32[]{:S(2)}) copy-start(bf16[2,128,512]{2,1,0:T(8,128)(2,1)S(1)} %constant_dynamic-slice_fusion.3) | copy-start | bytes 786436
  95.1 16.6 %copy-start.40 = (f32[256,256]{0,1:T(8,128)}, f32[256,256]{0,1:T(8,128)S(1)}, u32[]{:S(2)}) copy-start(f32[256,256]{0,1:T(8,128)S(1)} %get-tuple-element.81) | copy-start | bytes 786436
  95.4 85.0 %copy-start.8 = (bf16[4,64,512]{2,1,0:T(8,128)(2,1)}, bf16[4,64,512]{2,1,0:T(8,128)(2,1)S(1)}, u32[]{:S(2)}) copy-start(bf16[4,64,512]{2,1,0:T(8,128)(2,1)S(1)} %constant_dynamic-slice_fusion.2) | copy-start | bytes 786436
  96.1 79.8 %copy-start.9 = (bf16[8,32,512]{2,1,0:T(8,128)(2,1)}, bf16[8,32,512]{2,1,0:T(8,128)(2,1)S(1)}, u32[]{:S(2)}) copy-start(bf16[8,32,512]{2,1,0:T(8,128)(2,1)S(1)} %constant_dynamic-slice_fusion.1) | copy-start | bytes 786436
  96.6 132.2 %copy-start.6 = (bf16[16,16,512]{2,1,0:T(8,128)(2,1)}, bf16[16,16,512]{2,1,0:T(8,128)(2,1)S(1)}, u32[]{:S(2)}) copy-start(bf16[16,16,512]{2,1,0:T(8,128)(2,1)S(1)} %constant_dynamic-slice_fusion) | copy-start | bytes 786436
  97.9 19.6 %copy-start.82 = (f32[256]{0:T(256)}, f32[256]{0:T(256)S(1)}, u32[]{:S(2)}) copy-start(f32[256]{0:T(256)S(1)} %fusion.195) | copy-start | bytes 3076
  97.9 17.9 %copy-start.84 = (f32[256]{0:T(256)}, f32[256]{0:T(256)S(1)}, u32[]{:S(2)}) copy-start(f32[256]{0:T(256)S(1)} %fusion.203) | copy-start | bytes 3076
  117.5 48.9 %copy-start.28 = (f32[256,128]{0,1:T(8,128)}, f32[256,128]{0,1:T(8,128)S(1)}, u32[]{:S(2)}) copy-start(f32[256,128]{0,1:T(8,128)S(1)} %get-tuple-element.86) | copy-start | bytes 393220
  119.1 47.3 %copy-start.29 = (f32[256,128]{0,1:T(8,128)}, f32[256,128]{0,1:T(8,128)S(1)}, u32[]{:S(2)}) copy-start(f32[256,128]{0,1:T(8,128)S(1)} %get-tuple-element.84) | copy-start | bytes 393220
  175.8 13.4 %copy-start.21 = (bf16[256,256]{0,1:T(8,128)(2,1)}, bf16[256,256]{0,1:T(8,128)(2,1)S(1)}, u32[]{:S(2)}) copy-start(bf16[256,256]{0,1:T(8,128)(2,1)S(1)} %fusion.51) | copy-start | bytes 393220
  176.8 13.2 %copy-start.16 = (bf16[256,256]{0,1:T(8,128)(2,1)}, bf16[256,256]{0,1:T(8,128)(2,1)S(1)}, u32[]{:S(2)}) copy-start(bf16[256,256]{0,1:T(8,128)(2,1)S(1)} %fusion.56) | copy-start | bytes 393220
  177.7 13.2 %copy-start.17 = (bf16[256,256]{0,1:T(8,128)(2,1)}, bf16[256,256]{0,1:T(8,128)(2,1)S(1)}, u32[]{:S(2)}) copy-start(bf16[256,256]{0,1:T(8,128)(2,1)S(1)} %fusion.52) | copy-start | bytes 393220
  180.5 15.9 %copy-start.25 = (bf16[256,256]{0,1:T(8,128)(2,1)}, bf16[256,256]{0,1:T(8,128)(2,1)S(1)}, u32[]{:S(2)}) copy-start(bf16[256,256]{0,1:T(8,128)(2,1)S(1)} %fusion.49) | copy-start | bytes 393220
  181.2 16.0 %copy-start.23 = (bf16[256,256]{0,1:T(8,128)(2,1)}, bf16[256,256]{0,1:T(8,128)(2,1)S(1)}, u32[]{:S(2)}) copy-start(bf16[256,256]{0,1:T(8,128)(2,1)S(1)} %fusion.54) | copy-start | bytes 393220
  183.2 14.8 %copy-start.27 = (bf16[256,256]{0,1:T(8,128)(2,1)}, bf16[256,256]{0,1:T(8,128)(2,1)S(1)}, u32[]{:S(2)}) copy-start(bf16[256,256]{0,1:T(8,128)(2,1)S(1)} %fusion.48) | copy-start | bytes 393220
  183.5 15.4 %copy-start.26 = (bf16[256,256]{0,1:T(8,128)(2,1)}, bf16[256,256]{0,1:T(8,128)(2,1)S(1)}, u32[]{:S(2)}) copy-start(bf16[256,256]{0,1:T(8,128)(2,1)S(1)} %fusion.53) | copy-start | bytes 393220
  191.9 42.6 %collective-permute-start.4 = (bf16[128,512]{1,0:T(8,128)(2,1)}, bf16[128,512]{1,0:T(8,128)(2,1)}, u32[]{:S(2)}, u32[]{:S(2)}) collective-permute-start(bf16[128,512]{1,0:T(8,128)(2,1)} %select_convert_fusion), channel_id=1, source_target_pairs={{0,256},{16,272},{32,288},{48,304},{64,320},{80,336},{96,352},{112... | collective-permute-start | bytes 393224 | tf_op jit(solution)/shard_map/ppermute | solution.py:52
  204.3 21.1 %copy-start.12 = (f32[2,128,128]{2,1,0:T(8,128)S(1)}, f32[2,128,128]{2,1,0:T(8,128)}, u32[]{:S(2)}) copy-start(f32[2,128,128]{2,1,0:T(8,128)} %fusion.289) | copy-start | bytes 393220
  205.6 24.4 %copy-start.13 = (f32[2,128,128]{2,1,0:T(8,128)S(1)}, f32[2,128,128]{2,1,0:T(8,128)}, u32[]{:S(2)}) copy-start(f32[2,128,128]{2,1,0:T(8,128)} %fusion.290) | copy-start | bytes 393220
  205.6 72.5 %collective-permute-start.2 = (bf16[256,512]{1,0:T(8,128)(2,1)}, bf16[256,512]{1,0:T(8,128)(2,1)}, u32[]{:S(2)}, u32[]{:S(2)}) collective-permute-start(bf16[256,512]{1,0:T(8,128)(2,1)} %convert_element_type.240), channel_id=1, source_target_pairs={{16,0},{32,16},{48,32},{64,48},{80,64},{96,80},{112,96},{128,112},... | collective-permute-start | bytes 786440 | tf_op jit(solution)/shard_map/ppermute | solution.py:38
  223.3 54.8 %collective-permute-start.3 = (bf16[256,512]{1,0:T(8,128)(2,1)}, bf16[256,512]{1,0:T(8,128)(2,1)}, u32[]{:S(2)}, u32[]{:S(2)}) collective-permute-start(bf16[256,512]{1,0:T(8,128)(2,1)} %convert_element_type.242), channel_id=1, source_target_pairs={{0,16},{16,32},{32,48},{48,64},{64,80},{80,96},{96,112},{112,128},... | collective-permute-start | bytes 786440 | tf_op jit(solution)/shard_map/ppermute | solution.py:38
  235.7 7.1 %collective-permute-start.5 = (bf16[192,512]{1,0:T(8,128)(2,1)S(1)}, bf16[192,512]{1,0:T(8,128)(2,1)S(1)}, u32[]{:S(2)}, u32[]{:S(2)}) collective-permute-start(bf16[192,512]{1,0:T(8,128)(2,1)S(1)} %pad_maximum_fusion.10), channel_id=1, source_target_pairs={{0,128},{16,144},{32,160},{48,176},{64,192},{80,208},{96,224},{112... | collective-permute-start | bytes 589832 | tf_op jit(solution)/shard_map/ppermute | solution.py:52
  242.9 15.9 %copy-start.18 = (bf16[256,256]{0,1:T(8,128)(2,1)S(1)}, bf16[256,256]{0,1:T(8,128)(2,1)}, u32[]{:S(2)}) copy-start(bf16[256,256]{0,1:T(8,128)(2,1)} %copy-done.17) | copy-start | bytes 393220
  243.0 9.9 %collective-permute-start.6 = (bf16[224,512]{1,0:T(8,128)(2,1)S(1)}, bf16[224,512]{1,0:T(8,128)(2,1)S(1)}, u32[]{:S(2)}, u32[]{:S(2)}) collective-permute-start(bf16[224,512]{1,0:T(8,128)(2,1)S(1)} %pad_maximum_fusion.9), channel_id=1, source_target_pairs={{0,64},{16,80},{32,96},{48,112},{64,0},{80,16},{96,32},{112,48},{1... | collective-permute-start | bytes 688136 | tf_op jit(solution)/shard_map/ppermute | solution.py:52
  253.0 14.0 %copy-start.5 = (f32[64,512]{1,0:T(8,128)}, f32[64,512]{1,0:T(8,128)S(1)}, u32[]{:S(2)}) copy-start(f32[64,512]{1,0:T(8,128)S(1)} %convert_add_fusion.5) | copy-start | bytes 393220
  253.0 13.0 %copy-start.4 = (f32[256,512]{1,0:T(8,128)S(1)}, f32[256,512]{1,0:T(8,128)}, u32[]{:S(2)}) copy-start(f32[256,512]{1,0:T(8,128)} %copy-done.3) | copy-start | bytes 1572868
  253.8 12.2 %collective-permute-start.7 = (bf16[240,512]{1,0:T(8,128)(2,1)}, bf16[240,512]{1,0:T(8,128)(2,1)}, u32[]{:S(2)}, u32[]{:S(2)}) collective-permute-start(bf16[240,512]{1,0:T(8,128)(2,1)} %pad_maximum_fusion.8), channel_id=1, source_target_pairs={{0,32},{16,48},{32,0},{48,16},{64,96},{80,112},{96,64},{112,80},{1... | collective-permute-start | bytes 737288 | tf_op jit(solution)/shard_map/ppermute | solution.py:52
  261.5 13.8 %copy-start.15 = (bf16[256,256]{0,1:T(8,128)(2,1)S(1)}, bf16[256,256]{0,1:T(8,128)(2,1)}, u32[]{:S(2)}) copy-start(bf16[256,256]{0,1:T(8,128)(2,1)} %copy-done.14) | copy-start | bytes 393220
  261.5 14.9 %copy-start.66 = (bf16[256,128]{1,0:T(8,128)(2,1)S(1)}, bf16[256,128]{1,0:T(8,128)(2,1)}, u32[]{:S(2)}) copy-start(bf16[256,128]{1,0:T(8,128)(2,1)} %fusion.61) | copy-start | bytes 196612
  271.9 5.2 %collective-permute-start.8 = (bf16[248,512]{1,0:T(8,128)(2,1)}, bf16[248,512]{1,0:T(8,128)(2,1)S(1)}, u32[]{:S(2)}, u32[]{:S(2)}) collective-permute-start(bf16[248,512]{1,0:T(8,128)(2,1)} %constant_dynamic-update-slice_fusion.4), channel_id=1, source_target_pairs={{0,16},{16,0},{32,48},{48,32},{64,80},{80,64},{96,112},{112,96},{1... | collective-permute-start | bytes 761864 | tf_op jit(solution)/shard_map/ppermute | solution.py:52
  (116 other events, 465.4 us)
Sparse Core Ops, SparseCore 0:
  13.6 73.3 all-gather.3
